TPU v7x, 256 devices: a whole 4x4x8 slice. The times are simulated.
256 devices in a mesh: section: 8 (over x, core), tm: 32 (over y, z).
Axes of the slice: x: 4, y: 4, z: 8, core: 2. Of those that a mesh axis runs over, the one named last changes fastest.
Arguments:
- frames: bfloat16 [4, 4096, 2048], P(None, 'tm'), may hold values from -6 to 6
- norm_gain: bfloat16 [8, 2048], P('section'), may hold values from 0.5 to 1.5
- w_qkv: bfloat16 [8, 2048, 3072], P('section', 'tm'), may hold values from -8 to 8
- w_out: bfloat16 [8, 1024, 2048], P('section', 'tm'), may hold values from -0.1875 to 0.1875
- lengths: int32 [4, 1], replicated, may hold values from 1365 to 4096, as said below
- windows: int32 [8], replicated, may hold values from 32 to 64, as said below
- shifts: int32 [8], replicated, may hold values from 0 to 63, as said below
Outputs:
- hidden: bfloat16 [8, 4, 4096, 2048], P('section', None, 'tm')
Inputs may be any that keep to these rules, and one draw needn't show every extreme that they name: `lengths`: some micro-batch fills all 4096 frames of its slot. `windows`: some layer has a window of exactly 64. `shifts`: each below its layer's window; some layer shifts by 0 and some by 64 - 1.
All inputs are finite; a program needn't handle non-finite values.
Results may differ from a plain program's by a relative error of at most 0.024.
Values may be sent and summed in bfloat16 or wider, within the bound.
A program may use at most 64 MiB of HBM per device.

v0:
```python
import math

import jax
import jax.numpy as jnp
from jax import lax
from jax.sharding import PartitionSpec as P

HDIM = 128
WMAX = 64


def extended(cells, sides, width):
    for axis, dim in sides:
        count = lax.axis_size(axis)
        ends = count - 1
        head = lax.slice_in_dim(cells, 0, width, axis=dim)
        tail = lax.slice_in_dim(cells, cells.shape[dim] - width, cells.shape[dim], axis=dim)
        cells = jnp.concatenate(
            [
                lax.ppermute(tail, axis, [(i, (i + 1) % count) for i in range(ends)]),
                cells,
                lax.ppermute(head, axis, [((i + 1) % count, i) for i in range(ends)]),
            ],
            axis=dim,
        )
    return cells


def from_behind(block, axis, distance):
    devices = range(lax.axis_size(axis))
    route = [(i - distance, i) for i in devices if i - distance in devices]
    return lax.ppermute(block, axis, route)


def on_device(frames, norm_gain, w_qkv, w_out, lengths, windows, shifts):
    section_id = lax.axis_index("section")
    section_count = lax.axis_size("section")
    position = lax.axis_index("tm")
    tm_count = lax.axis_size("tm")
    micro_count = frames.shape[0]
    frame_rows = frames.shape[1]
    model_width = frames.shape[2]
    qkv_full, out_full = (
        lax.all_gather(w_qkv[0], "tm", axis=0, tiled=True),
        lax.all_gather(w_out[0], "tm", axis=0, tiled=True),
    )
    head_width = out_full.shape[0]
    head_count = head_width // HDIM
    slot_count = lengths.shape[1]
    total_frames = frame_rows * tm_count
    capacity = total_frames // slot_count
    window = windows[section_id]
    offset = shifts[section_id]
    norm_scale = norm_gain[0].astype(jnp.float32)
    margin = WMAX
    scale = 1.0 / math.sqrt(HDIM)
    query_pos = position * frame_rows + jnp.arange(frame_rows, dtype=jnp.int32)
    key_pos = position * frame_rows - margin + jnp.arange(frame_rows + 2 * margin, dtype=jnp.int32)

    def valid_at(indices, slot_lengths):
        slot_index = jnp.floor_divide(indices, capacity)
        clipped = jnp.clip(slot_index, 0, slot_count - 1)
        match = clipped[:, None] == jnp.arange(slot_count, dtype=jnp.int32)[None, :]
        length_of = jnp.sum(jnp.where(match, slot_lengths[None, :], 0), axis=1)
        inside = (indices >= 0) & (indices < total_frames)
        return (inside & (indices - slot_index * capacity < length_of), slot_index)

    def apply_layer(layer_input, micro_index, active):
        slot_lengths = lax.dynamic_index_in_dim(lengths, micro_index, 0, keepdims=False)
        query_valid, query_slot = valid_at(query_pos, slot_lengths)
        key_valid, key_slot = valid_at(key_pos, slot_lengths)
        input_wide = layer_input.astype(jnp.float32)
        centre = jnp.mean(input_wide, axis=-1, keepdims=True)
        centered = input_wide - centre
        variance = jnp.mean(centered * centered, axis=-1, keepdims=True)
        normed = (centered * lax.rsqrt(variance + 1e-05) * norm_scale).astype(jnp.bfloat16)
        projected = lax.cond(
            active,
            lambda: jnp.dot(normed, qkv_full, preferred_element_type=jnp.float32).astype(
                jnp.bfloat16
            ),
            lambda: jnp.zeros((frame_rows, 3 * head_width), jnp.bfloat16),
        )
        queries = projected[:, :head_width]
        keyval = extended(projected[:, head_width:], (("tm", 0),), margin)

        def attend():
            query_heads = queries.reshape(frame_rows, head_count, HDIM)
            key_heads = keyval[:, :head_width].reshape(-1, head_count, HDIM)
            value_heads = keyval[:, head_width:].reshape(-1, head_count, HDIM)
            scores = (
                jnp.einsum(
                    "qhd,khd->hqk", query_heads, key_heads, preferred_element_type=jnp.float32
                )
                * scale
            )
            same_window = (
                jnp.floor_divide(query_pos - offset, window)[:, None]
                == jnp.floor_divide(key_pos - offset, window)[None, :]
            )
            allowed = (
                (query_slot[:, None] == key_slot[None, :])
                & same_window
                & (key_valid[None, :] | (query_pos[:, None] == key_pos[None, :]))
            )
            scores = jnp.where(allowed[None], scores, -1e30)
            row_max = jnp.max(scores, axis=-1, keepdims=True)
            weights = jnp.where(allowed[None], jnp.exp(scores - row_max), 0.0)
            probability = (weights / jnp.sum(weights, axis=-1, keepdims=True)).astype(jnp.bfloat16)
            mixed = jnp.einsum(
                "hqk,khd->qhd", probability, value_heads, preferred_element_type=jnp.float32
            )
            mixed = mixed.astype(jnp.bfloat16).reshape(frame_rows, head_width)
            projection = jnp.dot(mixed, out_full, preferred_element_type=jnp.float32)
            return (input_wide + query_valid[:, None].astype(jnp.float32) * projection).astype(
                jnp.bfloat16
            )

        return lax.cond(active, attend, lambda: layer_input)

    def advance(time_step, carry):
        previous, stored = carry
        received = from_behind(previous, "section", 1)
        micro_index = time_step - section_id
        active = (micro_index >= 0) & (micro_index < micro_count)
        clipped = jnp.clip(micro_index, 0, micro_count - 1)
        entry_frames = lax.dynamic_index_in_dim(frames, clipped, 0, keepdims=False)
        layer_input = jnp.where(section_id == 0, entry_frames, received)
        result = apply_layer(layer_input, clipped, active)
        updated = lax.dynamic_update_index_in_dim(stored, result, clipped, 0)
        stored = jnp.where(active, updated, stored)
        return (result, stored)

    start_state = (
        jnp.zeros((frame_rows, model_width), jnp.bfloat16),
        jnp.zeros((micro_count, frame_rows, model_width), jnp.bfloat16),
    )
    final = lax.fori_loop(0, micro_count + section_count - 1, advance, start_state)
    return final[1][None]


def solution(mesh):
    return jax.shard_map(
        on_device,
        mesh=mesh,
        in_specs=(
            P(None, "tm", None),
            P("section", None),
            P("section", "tm", None),
            P("section", "tm", None),
            P(),
            P(),
            P(),
        ),
        out_specs=P("section", None, "tm", None),
        check_vma=False,
    )
```

profile of v0, /device:TPU:15, one launch (start us, length us, event | category | flops | bytes accessed | tf_op | source)
XLA Modules:
  0.0 813.7 jit_solution(15209331428826663283)
XLA Ops:
  11.3 79.2 %all-gather.7.cloned.1.call-done = bf16[1,1024,2048]{2,1,0:T(8,128)(2,1)} async-done(((bf16[1,32,2048]{2,1,0:T(8,128)(2,1)}), bf16[1,1024,2048]{2,1,0:T(8,128)(2,1)}) %all-gather.7.cloned.1.call-update) | async-done | bytes 4194320 | tf_op jit(solution)/shard_map/all_gather | solution.py:45
  90.6 121.9 %all-gather.5.cloned.1.call-done = bf16[1,2048,3072]{2,1,0:T(8,128)(2,1)} async-done(((bf16[1,64,3072]{2,1,0:T(8,128)(2,1)}), bf16[1,2048,3072]{2,1,0:T(8,128)(2,1)}) %all-gather.5.cloned.1.call-update) | async-done | bytes 12582928 | tf_op jit(solution)/shard_map/all_gather | solution.py:44
  214.1 592.8 %while.20 = (s32[]{:T(128)}, bf16[128,2048]{1,0:T(8,128)(2,1)S(1)}, bf16[4,128,2048]{2,1,0:T(8,128)(2,1)}, s32[]{:T(128)}, pred[]{:T(512)}, /*index=5*/bf16[4,12...) while((s32[]{:T(128)}, bf16[128,2048]{1,0:T(8,128)(2,1)S(1)}, ...), condition=%wide.region_9.10_spmd.clone.clone, body=%wide.region_0.9_spmd.clone.clone.sunk | while | flops 2360033280 | bytes 49722760 | solution.py:138
  215.4 3.1 collective-permute-done
  224.5 5.5 collective-permute-start.1
  231.2 3.7 collective-permute-done.2
  241.7 10.3 %collective-permute-done = bf16[128,2048]{1,0:T(8,128)(2,1)S(1)} collective-permute-done((bf16[128,2048]{1,0:T(8,128)(2,1)S(1)}, bf16[128,2048]{1,0:T(8,128)(2,1)S(1)}, u32[]{:S(2)}, u32[]{:S(2)}) %collective-permute-start) | collective-permute-done | bytes 524320 | tf_op jit(solution)/shard_map/while/body/eval_jaxpr/ppermute | solution.py:32
  258.3 6.1 collective-permute-start.1
  265.5 3.7 collective-permute-done.2
  276.0 10.0 %collective-permute-done = bf16[128,2048]{1,0:T(8,128)(2,1)S(1)} collective-permute-done((bf16[128,2048]{1,0:T(8,128)(2,1)S(1)}, bf16[128,2048]{1,0:T(8,128)(2,1)S(1)}, u32[]{:S(2)}, u32[]{:S(2)}) %collective-permute-start) | collective-permute-done | bytes 524320 | tf_op jit(solution)/shard_map/while/body/eval_jaxpr/ppermute | solution.py:32
  292.2 6.2 collective-permute-start.1
  299.5 3.7 collective-permute-done.2
  310.1 10.0 %collective-permute-done = bf16[128,2048]{1,0:T(8,128)(2,1)S(1)} collective-permute-done((bf16[128,2048]{1,0:T(8,128)(2,1)S(1)}, bf16[128,2048]{1,0:T(8,128)(2,1)S(1)}, u32[]{:S(2)}, u32[]{:S(2)}) %collective-permute-start) | collective-permute-done | bytes 524320 | tf_op jit(solution)/shard_map/while/body/eval_jaxpr/ppermute | solution.py:32
  326.2 6.2 collective-permute-start.1
  333.5 3.7 collective-permute-done.2
  344.1 10.0 %collective-permute-done = bf16[128,2048]{1,0:T(8,128)(2,1)S(1)} collective-permute-done((bf16[128,2048]{1,0:T(8,128)(2,1)S(1)}, bf16[128,2048]{1,0:T(8,128)(2,1)S(1)}, u32[]{:S(2)}, u32[]{:S(2)}) %collective-permute-start) | collective-permute-done | bytes 524320 | tf_op jit(solution)/shard_map/while/body/eval_jaxpr/ppermute | solution.py:32
  360.2 6.2 collective-permute-start.1
  367.5 3.7 collective-permute-done.2
  378.1 10.0 %collective-permute-done = bf16[128,2048]{1,0:T(8,128)(2,1)S(1)} collective-permute-done((bf16[128,2048]{1,0:T(8,128)(2,1)S(1)}, bf16[128,2048]{1,0:T(8,128)(2,1)S(1)}, u32[]{:S(2)}, u32[]{:S(2)}) %collective-permute-start) | collective-permute-done | bytes 524320 | tf_op jit(solution)/shard_map/while/body/eval_jaxpr/ppermute | solution.py:32
  394.2 6.2 collective-permute-start.1
  401.6 3.7 collective-permute-done.2
  412.1 10.0 %collective-permute-done = bf16[128,2048]{1,0:T(8,128)(2,1)S(1)} collective-permute-done((bf16[128,2048]{1,0:T(8,128)(2,1)S(1)}, bf16[128,2048]{1,0:T(8,128)(2,1)S(1)}, u32[]{:S(2)}, u32[]{:S(2)}) %collective-permute-start) | collective-permute-done | bytes 524320 | tf_op jit(solution)/shard_map/while/body/eval_jaxpr/ppermute | solution.py:32
  428.2 6.2 collective-permute-start.1
  435.6 3.7 collective-permute-done.2
  446.2 135.9 %collective-permute-done = bf16[128,2048]{1,0:T(8,128)(2,1)S(1)} collective-permute-done((bf16[128,2048]{1,0:T(8,128)(2,1)S(1)}, bf16[128,2048]{1,0:T(8,128)(2,1)S(1)}, u32[]{:S(2)}, u32[]{:S(2)}) %collective-permute-start) | collective-permute-done | bytes 524320 | tf_op jit(solution)/shard_map/while/body/eval_jaxpr/ppermute | solution.py:32
  584.1 6.4 conditional.8
  584.1 6.4 convolution_convert_fusion
  594.4 6.2 collective-permute-start.1
  601.8 3.7 collective-permute-done.2
  609.1 15.4 %conditional.9 = (bf16[128,2048]{1,0:T(8,128)(2,1)S(1)}) conditional(s32[]{:T(128)} %convert_element_type.106, bf16[128,2048]{1,0:T(8,128)(2,1)S(1)} %get-tuple-element.1246, (s32[128]{0:T(128)S(1)}, s32[128]{0:T(128)S(1)}, s32[128]{0:T(128)S(1)}, s32[]{:T(128)}, s32[128]{0:T(128)S(1)}, /*index=5*/pred[128]{0:T(512)(128)(4,1)S(1)}, ...), branch_computations={%region_5.5_spmd, %region_6.8_spmd.clone} | conditional | flops 742209152 | bytes 17984388 | solution.py:119
  627.8 10.0 %collective-permute-done = bf16[128,2048]{1,0:T(8,128)(2,1)S(1)} collective-permute-done((bf16[128,2048]{1,0:T(8,128)(2,1)S(1)}, bf16[128,2048]{1,0:T(8,128)(2,1)S(1)}, u32[]{:S(2)}, u32[]{:S(2)}) %collective-permute-start) | collective-permute-done | bytes 524320 | tf_op jit(solution)/shard_map/while/body/eval_jaxpr/ppermute | solution.py:32
  639.8 6.4 conditional.8
  639.8 6.4 convolution_convert_fusion
  650.2 6.2 collective-permute-start.1
  657.5 3.7 collective-permute-done.2
  664.8 15.4 %conditional.9 = (bf16[128,2048]{1,0:T(8,128)(2,1)S(1)}) conditional(s32[]{:T(128)} %convert_element_type.106, bf16[128,2048]{1,0:T(8,128)(2,1)S(1)} %get-tuple-element.1246, (s32[128]{0:T(128)S(1)}, s32[128]{0:T(128)S(1)}, s32[128]{0:T(128)S(1)}, s32[]{:T(128)}, s32[128]{0:T(128)S(1)}, /*index=5*/pred[128]{0:T(512)(128)(4,1)S(1)}, ...), branch_computations={%region_5.5_spmd, %region_6.8_spmd.clone} | conditional | flops 742209152 | bytes 17984388 | solution.py:119
  683.5 10.0 %collective-permute-done = bf16[128,2048]{1,0:T(8,128)(2,1)S(1)} collective-permute-done((bf16[128,2048]{1,0:T(8,128)(2,1)S(1)}, bf16[128,2048]{1,0:T(8,128)(2,1)S(1)}, u32[]{:S(2)}, u32[]{:S(2)}) %collective-permute-start) | collective-permute-done | bytes 524320 | tf_op jit(solution)/shard_map/while/body/eval_jaxpr/ppermute | solution.py:32
  695.5 6.4 conditional.8
  695.5 6.4 convolution_convert_fusion
  705.9 6.2 collective-permute-start.1
  713.3 3.7 collective-permute-done.2
  720.5 15.4 %conditional.9 = (bf16[128,2048]{1,0:T(8,128)(2,1)S(1)}) conditional(s32[]{:T(128)} %convert_element_type.106, bf16[128,2048]{1,0:T(8,128)(2,1)S(1)} %get-tuple-element.1246, (s32[128]{0:T(128)S(1)}, s32[128]{0:T(128)S(1)}, s32[128]{0:T(128)S(1)}, s32[]{:T(128)}, s32[128]{0:T(128)S(1)}, /*index=5*/pred[128]{0:T(512)(128)(4,1)S(1)}, ...), branch_computations={%region_5.5_spmd, %region_6.8_spmd.clone} | conditional | flops 742209152 | bytes 17984388 | solution.py:119
  739.2 19.0 %collective-permute-done = bf16[128,2048]{1,0:T(8,128)(2,1)S(1)} collective-permute-done((bf16[128,2048]{1,0:T(8,128)(2,1)S(1)}, bf16[128,2048]{1,0:T(8,128)(2,1)S(1)}, u32[]{:S(2)}, u32[]{:S(2)}) %collective-permute-start) | collective-permute-done | bytes 524320 | tf_op jit(solution)/shard_map/while/body/eval_jaxpr/ppermute | solution.py:32
  760.3 6.4 conditional.8
  760.3 6.4 convolution_convert_fusion
  770.7 6.2 collective-permute-start.1
  778.0 8.5 %collective-permute-done.2 = bf16[64,2048]{0,1:T(8,128)(2,1)S(1)} collective-permute-done((bf16[64,2048]{0,1:T(8,128)(2,1)}, bf16[64,2048]{0,1:T(8,128)(2,1)S(1)}, u32[]{:S(2)}, u32[]{:S(2)}) %collective-permute-start.2) | collective-permute-done | bytes 262176 | tf_op jit(solution)/shard_map/while/body/eval_jaxpr/ppermute | solution.py:20
  789.5 15.4 %conditional.9 = (bf16[128,2048]{1,0:T(8,128)(2,1)S(1)}) conditional(s32[]{:T(128)} %convert_element_type.106, bf16[128,2048]{1,0:T(8,128)(2,1)S(1)} %get-tuple-element.1246, (s32[128]{0:T(128)S(1)}, s32[128]{0:T(128)S(1)}, s32[128]{0:T(128)S(1)}, s32[]{:T(128)}, s32[128]{0:T(128)S(1)}, /*index=5*/pred[128]{0:T(512)(128)(4,1)S(1)}, ...), branch_computations={%region_5.5_spmd, %region_6.8_spmd.clone} | conditional | flops 742209152 | bytes 17984388 | solution.py:119
  (364 shorter events, 218.2 us)
Async XLA Ops:
  6.5 207.6 %copy-start.3 = (s32[4,1]{0,1:T(1,128)S(1)}, s32[4,1]{0,1:T(1,128)}, u32[]{:S(2)}) copy-start(s32[4,1]{0,1:T(1,128)} %param.17) | copy-start | bytes 52
  6.5 84.0 %all-gather.7.cloned.1.call-start = ((), (), s32[]{:S(2)}) async-start(), calls=%async_computation.1 | async-start | bytes 4325376 | tf_op jit(solution)/shard_map/all_gather | solution.py:45
  7.3 205.2 %all-gather.5.cloned.1.call-start = ((), (), s32[]{:S(2)}) async-start(), calls=%async_computation | async-start | bytes 12976128 | tf_op jit(solution)/shard_map/all_gather | solution.py:44
  214.1 4.4 collective-permute-start
  222.6 12.2 %collective-permute-start.2 = (bf16[64,2048]{0,1:T(8,128)(2,1)}, bf16[64,2048]{0,1:T(8,128)(2,1)S(1)}, u32[]{:S(2)}, u32[]{:S(2)}) collective-permute-start(bf16[64,2048]{0,1:T(8,128)(2,1)} %copy.28), channel_id=1, source_target_pairs={{0,1},{1,2},{2,3},{3,4},{4,5},{5,6},{6,7},{7,8},{8,9},{9,10},{10,1... | collective-permute-start | bytes 786440 | tf_op jit(solution)/shard_map/while/body/eval_jaxpr/ppermute | solution.py:20
  224.5 11.9 %collective-permute-start.1 = (bf16[64,2048]{0,1:T(8,128)(2,1)}, bf16[64,2048]{0,1:T(8,128)(2,1)}, u32[]{:S(2)}, u32[]{:S(2)}) collective-permute-start(bf16[64,2048]{0,1:T(8,128)(2,1)} %copy.26), channel_id=1, source_target_pairs={{1,0},{2,1},{3,2},{4,3},{5,4},{6,5},{7,6},{8,7},{9,8},{10,9},{11,1... | collective-permute-start | bytes 786440 | tf_op jit(solution)/shard_map/while/body/eval_jaxpr/ppermute | solution.py:22
  234.9 0.8 copy-start.1
  240.4 11.6 %collective-permute-start = (bf16[128,2048]{1,0:T(8,128)(2,1)S(1)}, bf16[128,2048]{1,0:T(8,128)(2,1)S(1)}, u32[]{:S(2)}, u32[]{:S(2)}) collective-permute-start(bf16[128,2048]{1,0:T(8,128)(2,1)S(1)} %get-tuple-element.1274), channel_id=1, source_target_pairs={{0,32},{32,64},{64,96},{96,128},{128,160},{160,192},{192,224},{1,3... | collective-permute-start | bytes 1572872 | tf_op jit(solution)/shard_map/while/body/eval_jaxpr/ppermute | solution.py:32
  256.2 13.0 %collective-permute-start.2 = (bf16[64,2048]{0,1:T(8,128)(2,1)}, bf16[64,2048]{0,1:T(8,128)(2,1)S(1)}, u32[]{:S(2)}, u32[]{:S(2)}) collective-permute-start(bf16[64,2048]{0,1:T(8,128)(2,1)} %copy.28), channel_id=1, source_target_pairs={{0,1},{1,2},{2,3},{3,4},{4,5},{5,6},{6,7},{7,8},{8,9},{9,10},{10,1... | collective-permute-start | bytes 786440 | tf_op jit(solution)/shard_map/while/body/eval_jaxpr/ppermute | solution.py:20
  258.3 12.5 %collective-permute-start.1 = (bf16[64,2048]{0,1:T(8,128)(2,1)}, bf16[64,2048]{0,1:T(8,128)(2,1)}, u32[]{:S(2)}, u32[]{:S(2)}) collective-permute-start(bf16[64,2048]{0,1:T(8,128)(2,1)} %copy.26), channel_id=1, source_target_pairs={{1,0},{2,1},{3,2},{4,3},{5,4},{6,5},{7,6},{8,7},{9,8},{10,9},{11,1... | collective-permute-start | bytes 786440 | tf_op jit(solution)/shard_map/while/body/eval_jaxpr/ppermute | solution.py:22
  274.7 11.3 %collective-permute-start = (bf16[128,2048]{1,0:T(8,128)(2,1)S(1)}, bf16[128,2048]{1,0:T(8,128)(2,1)S(1)}, u32[]{:S(2)}, u32[]{:S(2)}) collective-permute-start(bf16[128,2048]{1,0:T(8,128)(2,1)S(1)} %get-tuple-element.1274), channel_id=1, source_target_pairs={{0,32},{32,64},{64,96},{96,128},{128,160},{160,192},{192,224},{1,3... | collective-permute-start | bytes 1572872 | tf_op jit(solution)/shard_map/while/body/eval_jaxpr/ppermute | solution.py:32
  290.2 13.0 %collective-permute-start.2 = (bf16[64,2048]{0,1:T(8,128)(2,1)}, bf16[64,2048]{0,1:T(8,128)(2,1)S(1)}, u32[]{:S(2)}, u32[]{:S(2)}) collective-permute-start(bf16[64,2048]{0,1:T(8,128)(2,1)} %copy.28), channel_id=1, source_target_pairs={{0,1},{1,2},{2,3},{3,4},{4,5},{5,6},{6,7},{7,8},{8,9},{9,10},{10,1... | collective-permute-start | bytes 786440 | tf_op jit(solution)/shard_map/while/body/eval_jaxpr/ppermute | solution.py:20
  292.2 12.6 %collective-permute-start.1 = (bf16[64,2048]{0,1:T(8,128)(2,1)}, bf16[64,2048]{0,1:T(8,128)(2,1)}, u32[]{:S(2)}, u32[]{:S(2)}) collective-permute-start(bf16[64,2048]{0,1:T(8,128)(2,1)} %copy.26), channel_id=1, source_target_pairs={{1,0},{2,1},{3,2},{4,3},{5,4},{6,5},{7,6},{8,7},{9,8},{10,9},{11,1... | collective-permute-start | bytes 786440 | tf_op jit(solution)/shard_map/while/body/eval_jaxpr/ppermute | solution.py:22
  303.2 0.8 copy-start.1
  308.7 11.3 %collective-permute-start = (bf16[128,2048]{1,0:T(8,128)(2,1)S(1)}, bf16[128,2048]{1,0:T(8,128)(2,1)S(1)}, u32[]{:S(2)}, u32[]{:S(2)}) collective-permute-start(bf16[128,2048]{1,0:T(8,128)(2,1)S(1)} %get-tuple-element.1274), channel_id=1, source_target_pairs={{0,32},{32,64},{64,96},{96,128},{128,160},{160,192},{192,224},{1,3... | collective-permute-start | bytes 1572872 | tf_op jit(solution)/shard_map/while/body/eval_jaxpr/ppermute | solution.py:32
  324.2 13.0 %collective-permute-start.2 = (bf16[64,2048]{0,1:T(8,128)(2,1)}, bf16[64,2048]{0,1:T(8,128)(2,1)S(1)}, u32[]{:S(2)}, u32[]{:S(2)}) collective-permute-start(bf16[64,2048]{0,1:T(8,128)(2,1)} %copy.28), channel_id=1, source_target_pairs={{0,1},{1,2},{2,3},{3,4},{4,5},{5,6},{6,7},{7,8},{8,9},{9,10},{10,1... | collective-permute-start | bytes 786440 | tf_op jit(solution)/shard_map/while/body/eval_jaxpr/ppermute | solution.py:20
  326.2 12.6 %collective-permute-start.1 = (bf16[64,2048]{0,1:T(8,128)(2,1)}, bf16[64,2048]{0,1:T(8,128)(2,1)}, u32[]{:S(2)}, u32[]{:S(2)}) collective-permute-start(bf16[64,2048]{0,1:T(8,128)(2,1)} %copy.26), channel_id=1, source_target_pairs={{1,0},{2,1},{3,2},{4,3},{5,4},{6,5},{7,6},{8,7},{9,8},{10,9},{11,1... | collective-permute-start | bytes 786440 | tf_op jit(solution)/shard_map/while/body/eval_jaxpr/ppermute | solution.py:22
  342.8 11.3 %collective-permute-start = (bf16[128,2048]{1,0:T(8,128)(2,1)S(1)}, bf16[128,2048]{1,0:T(8,128)(2,1)S(1)}, u32[]{:S(2)}, u32[]{:S(2)}) collective-permute-start(bf16[128,2048]{1,0:T(8,128)(2,1)S(1)} %get-tuple-element.1274), channel_id=1, source_target_pairs={{0,32},{32,64},{64,96},{96,128},{128,160},{160,192},{192,224},{1,3... | collective-permute-start | bytes 1572872 | tf_op jit(solution)/shard_map/while/body/eval_jaxpr/ppermute | solution.py:32
  358.3 13.0 %collective-permute-start.2 = (bf16[64,2048]{0,1:T(8,128)(2,1)}, bf16[64,2048]{0,1:T(8,128)(2,1)S(1)}, u32[]{:S(2)}, u32[]{:S(2)}) collective-permute-start(bf16[64,2048]{0,1:T(8,128)(2,1)} %copy.28), channel_id=1, source_target_pairs={{0,1},{1,2},{2,3},{3,4},{4,5},{5,6},{6,7},{7,8},{8,9},{9,10},{10,1... | collective-permute-start | bytes 786440 | tf_op jit(solution)/shard_map/while/body/eval_jaxpr/ppermute | solution.py:20
  360.2 12.6 %collective-permute-start.1 = (bf16[64,2048]{0,1:T(8,128)(2,1)}, bf16[64,2048]{0,1:T(8,128)(2,1)}, u32[]{:S(2)}, u32[]{:S(2)}) collective-permute-start(bf16[64,2048]{0,1:T(8,128)(2,1)} %copy.26), channel_id=1, source_target_pairs={{1,0},{2,1},{3,2},{4,3},{5,4},{6,5},{7,6},{8,7},{9,8},{10,9},{11,1... | collective-permute-start | bytes 786440 | tf_op jit(solution)/shard_map/while/body/eval_jaxpr/ppermute | solution.py:22
  371.2 0.8 copy-start.1
  376.8 11.3 %collective-permute-start = (bf16[128,2048]{1,0:T(8,128)(2,1)S(1)}, bf16[128,2048]{1,0:T(8,128)(2,1)S(1)}, u32[]{:S(2)}, u32[]{:S(2)}) collective-permute-start(bf16[128,2048]{1,0:T(8,128)(2,1)S(1)} %get-tuple-element.1274), channel_id=1, source_target_pairs={{0,32},{32,64},{64,96},{96,128},{128,160},{160,192},{192,224},{1,3... | collective-permute-start | bytes 1572872 | tf_op jit(solution)/shard_map/while/body/eval_jaxpr/ppermute | solution.py:32
  392.3 13.0 %collective-permute-start.2 = (bf16[64,2048]{0,1:T(8,128)(2,1)}, bf16[64,2048]{0,1:T(8,128)(2,1)S(1)}, u32[]{:S(2)}, u32[]{:S(2)}) collective-permute-start(bf16[64,2048]{0,1:T(8,128)(2,1)} %copy.28), channel_id=1, source_target_pairs={{0,1},{1,2},{2,3},{3,4},{4,5},{5,6},{6,7},{7,8},{8,9},{9,10},{10,1... | collective-permute-start | bytes 786440 | tf_op jit(solution)/shard_map/while/body/eval_jaxpr/ppermute | solution.py:20
  394.2 12.6 %collective-permute-start.1 = (bf16[64,2048]{0,1:T(8,128)(2,1)}, bf16[64,2048]{0,1:T(8,128)(2,1)}, u32[]{:S(2)}, u32[]{:S(2)}) collective-permute-start(bf16[64,2048]{0,1:T(8,128)(2,1)} %copy.26), channel_id=1, source_target_pairs={{1,0},{2,1},{3,2},{4,3},{5,4},{6,5},{7,6},{8,7},{9,8},{10,9},{11,1... | collective-permute-start | bytes 786440 | tf_op jit(solution)/shard_map/while/body/eval_jaxpr/ppermute | solution.py:22
  405.3 0.8 copy-start.1
  410.8 11.3 %collective-permute-start = (bf16[128,2048]{1,0:T(8,128)(2,1)S(1)}, bf16[128,2048]{1,0:T(8,128)(2,1)S(1)}, u32[]{:S(2)}, u32[]{:S(2)}) collective-permute-start(bf16[128,2048]{1,0:T(8,128)(2,1)S(1)} %get-tuple-element.1274), channel_id=1, source_target_pairs={{0,32},{32,64},{64,96},{96,128},{128,160},{160,192},{192,224},{1,3... | collective-permute-start | bytes 1572872 | tf_op jit(solution)/shard_map/while/body/eval_jaxpr/ppermute | solution.py:32
  426.3 13.0 %collective-permute-start.2 = (bf16[64,2048]{0,1:T(8,128)(2,1)}, bf16[64,2048]{0,1:T(8,128)(2,1)S(1)}, u32[]{:S(2)}, u32[]{:S(2)}) collective-permute-start(bf16[64,2048]{0,1:T(8,128)(2,1)} %copy.28), channel_id=1, source_target_pairs={{0,1},{1,2},{2,3},{3,4},{4,5},{5,6},{6,7},{7,8},{8,9},{9,10},{10,1... | collective-permute-start | bytes 786440 | tf_op jit(solution)/shard_map/while/body/eval_jaxpr/ppermute | solution.py:20
  428.2 12.6 %collective-permute-start.1 = (bf16[64,2048]{0,1:T(8,128)(2,1)}, bf16[64,2048]{0,1:T(8,128)(2,1)}, u32[]{:S(2)}, u32[]{:S(2)}) collective-permute-start(bf16[64,2048]{0,1:T(8,128)(2,1)} %copy.26), channel_id=1, source_target_pairs={{1,0},{2,1},{3,2},{4,3},{5,4},{6,5},{7,6},{8,7},{9,8},{10,9},{11,1... | collective-permute-start | bytes 786440 | tf_op jit(solution)/shard_map/while/body/eval_jaxpr/ppermute | solution.py:22
  444.8 137.2 %collective-permute-start = (bf16[128,2048]{1,0:T(8,128)(2,1)S(1)}, bf16[128,2048]{1,0:T(8,128)(2,1)S(1)}, u32[]{:S(2)}, u32[]{:S(2)}) collective-permute-start(bf16[128,2048]{1,0:T(8,128)(2,1)S(1)} %get-tuple-element.1274), channel_id=1, source_target_pairs={{0,32},{32,64},{64,96},{96,128},{128,160},{160,192},{192,224},{1,3... | collective-permute-start | bytes 1572872 | tf_op jit(solution)/shard_map/while/body/eval_jaxpr/ppermute | solution.py:32
  592.5 13.0 %collective-permute-start.2 = (bf16[64,2048]{0,1:T(8,128)(2,1)}, bf16[64,2048]{0,1:T(8,128)(2,1)S(1)}, u32[]{:S(2)}, u32[]{:S(2)}) collective-permute-start(bf16[64,2048]{0,1:T(8,128)(2,1)} %copy.28), channel_id=1, source_target_pairs={{0,1},{1,2},{2,3},{3,4},{4,5},{5,6},{6,7},{7,8},{8,9},{9,10},{10,1... | collective-permute-start | bytes 786440 | tf_op jit(solution)/shard_map/while/body/eval_jaxpr/ppermute | solution.py:20
  594.4 12.7 %collective-permute-start.1 = (bf16[64,2048]{0,1:T(8,128)(2,1)}, bf16[64,2048]{0,1:T(8,128)(2,1)}, u32[]{:S(2)}, u32[]{:S(2)}) collective-permute-start(bf16[64,2048]{0,1:T(8,128)(2,1)} %copy.26), channel_id=1, source_target_pairs={{1,0},{2,1},{3,2},{4,3},{5,4},{6,5},{7,6},{8,7},{9,8},{10,9},{11,1... | collective-permute-start | bytes 786440 | tf_op jit(solution)/shard_map/while/body/eval_jaxpr/ppermute | solution.py:22
  616.7 0.9 copy-start
  617.6 2.0 copy-start.2
  626.5 11.3 %collective-permute-start = (bf16[128,2048]{1,0:T(8,128)(2,1)S(1)}, bf16[128,2048]{1,0:T(8,128)(2,1)S(1)}, u32[]{:S(2)}, u32[]{:S(2)}) collective-permute-start(bf16[128,2048]{1,0:T(8,128)(2,1)S(1)} %get-tuple-element.1274), channel_id=1, source_target_pairs={{0,32},{32,64},{64,96},{96,128},{128,160},{160,192},{192,224},{1,3... | collective-permute-start | bytes 1572872 | tf_op jit(solution)/shard_map/while/body/eval_jaxpr/ppermute | solution.py:32
  648.2 13.0 %collective-permute-start.2 = (bf16[64,2048]{0,1:T(8,128)(2,1)}, bf16[64,2048]{0,1:T(8,128)(2,1)S(1)}, u32[]{:S(2)}, u32[]{:S(2)}) collective-permute-start(bf16[64,2048]{0,1:T(8,128)(2,1)} %copy.28), channel_id=1, source_target_pairs={{0,1},{1,2},{2,3},{3,4},{4,5},{5,6},{6,7},{7,8},{8,9},{9,10},{10,1... | collective-permute-start | bytes 786440 | tf_op jit(solution)/shard_map/while/body/eval_jaxpr/ppermute | solution.py:20
  650.2 12.7 %collective-permute-start.1 = (bf16[64,2048]{0,1:T(8,128)(2,1)}, bf16[64,2048]{0,1:T(8,128)(2,1)}, u32[]{:S(2)}, u32[]{:S(2)}) collective-permute-start(bf16[64,2048]{0,1:T(8,128)(2,1)} %copy.26), channel_id=1, source_target_pairs={{1,0},{2,1},{3,2},{4,3},{5,4},{6,5},{7,6},{8,7},{9,8},{10,9},{11,1... | collective-permute-start | bytes 786440 | tf_op jit(solution)/shard_map/while/body/eval_jaxpr/ppermute | solution.py:22
  672.5 0.9 copy-start
  673.3 2.0 copy-start.2
  682.2 11.3 %collective-permute-start = (bf16[128,2048]{1,0:T(8,128)(2,1)S(1)}, bf16[128,2048]{1,0:T(8,128)(2,1)S(1)}, u32[]{:S(2)}, u32[]{:S(2)}) collective-permute-start(bf16[128,2048]{1,0:T(8,128)(2,1)S(1)} %get-tuple-element.1274), channel_id=1, source_target_pairs={{0,32},{32,64},{64,96},{96,128},{128,160},{160,192},{192,224},{1,3... | collective-permute-start | bytes 1572872 | tf_op jit(solution)/shard_map/while/body/eval_jaxpr/ppermute | solution.py:32
  704.0 13.0 %collective-permute-start.2 = (bf16[64,2048]{0,1:T(8,128)(2,1)}, bf16[64,2048]{0,1:T(8,128)(2,1)S(1)}, u32[]{:S(2)}, u32[]{:S(2)}) collective-permute-start(bf16[64,2048]{0,1:T(8,128)(2,1)} %copy.28), channel_id=1, source_target_pairs={{0,1},{1,2},{2,3},{3,4},{4,5},{5,6},{6,7},{7,8},{8,9},{9,10},{10,1... | collective-permute-start | bytes 786440 | tf_op jit(solution)/shard_map/while/body/eval_jaxpr/ppermute | solution.py:20
  705.9 12.7 %collective-permute-start.1 = (bf16[64,2048]{0,1:T(8,128)(2,1)}, bf16[64,2048]{0,1:T(8,128)(2,1)}, u32[]{:S(2)}, u32[]{:S(2)}) collective-permute-start(bf16[64,2048]{0,1:T(8,128)(2,1)} %copy.26), channel_id=1, source_target_pairs={{1,0},{2,1},{3,2},{4,3},{5,4},{6,5},{7,6},{8,7},{9,8},{10,9},{11,1... | collective-permute-start | bytes 786440 | tf_op jit(solution)/shard_map/while/body/eval_jaxpr/ppermute | solution.py:22
  728.2 0.9 copy-start
  729.1 2.0 copy-start.2
  737.9 20.4 %collective-permute-start = (bf16[128,2048]{1,0:T(8,128)(2,1)S(1)}, bf16[128,2048]{1,0:T(8,128)(2,1)S(1)}, u32[]{:S(2)}, u32[]{:S(2)}) collective-permute-start(bf16[128,2048]{1,0:T(8,128)(2,1)S(1)} %get-tuple-element.1274), channel_id=1, source_target_pairs={{0,32},{32,64},{64,96},{96,128},{128,160},{160,192},{192,224},{1,3... | collective-permute-start | bytes 1572872 | tf_op jit(solution)/shard_map/while/body/eval_jaxpr/ppermute | solution.py:32
  768.7 17.8 %collective-permute-start.2 = (bf16[64,2048]{0,1:T(8,128)(2,1)}, bf16[64,2048]{0,1:T(8,128)(2,1)S(1)}, u32[]{:S(2)}, u32[]{:S(2)}) collective-permute-start(bf16[64,2048]{0,1:T(8,128)(2,1)} %copy.28), channel_id=1, source_target_pairs={{0,1},{1,2},{2,3},{3,4},{4,5},{5,6},{6,7},{7,8},{8,9},{9,10},{10,1... | collective-permute-start | bytes 786440 | tf_op jit(solution)/shard_map/while/body/eval_jaxpr/ppermute | solution.py:20
  770.7 16.9 %collective-permute-start.1 = (bf16[64,2048]{0,1:T(8,128)(2,1)}, bf16[64,2048]{0,1:T(8,128)(2,1)}, u32[]{:S(2)}, u32[]{:S(2)}) collective-permute-start(bf16[64,2048]{0,1:T(8,128)(2,1)} %copy.26), channel_id=1, source_target_pairs={{1,0},{2,1},{3,2},{4,3},{5,4},{6,5},{7,6},{8,7},{9,8},{10,9},{11,1... | collective-permute-start | bytes 786440 | tf_op jit(solution)/shard_map/while/body/eval_jaxpr/ppermute | solution.py:22
  797.2 0.9 copy-start
  798.0 2.0 copy-start.2
  (7 other events, 5.5 us)
Sparse Core Ops, SparseCore 0:
  9.9 80.5 all-gather.6
  93.1 119.2 all-gather.4
where the time goes:
time: 817 us; the launch traced here: 814 us
  waiting for transfers between devices  495 us (61%)
  starting transfers between devices  103 us (13%)
  other arithmetic  82.9 us (10%)
  local copies, waits for them, and re-layouts  62.4 us (8%)
  matrix products  52.9 us (6%)
  between operations  13.4 us (2%)
    ppermute x11, waiting for transfers between devices, from_behind(): return lax.ppermute(block, axis, route)  238 us
    all_gather x1, waiting for transfers between devices, on_device(): lax.all_gather(w_qkv[0], 'tm', axis=0, tiled=True)  122 us
    all_gather x1, waiting for transfers between devices, on_device(): lax.all_gather(w_out[0], 'tm', axis=0, tiled=True)  79.2 us
    ppermute x11, starting transfers between devices, extended(): lax.ppermute(head, axis, [((i + 1) % count, i) for i in range(ends)])  67.5 us
    ppermute x11, waiting for transfers between devices, extended(): lax.ppermute(tail, axis, [(i, (i + 1) % count) for i in range(ends)])  45.6 us
    while x55, local copies, waits for them, and re-layouts  42.3 us
    dot_general x4, matrix products, apply_layer(): jnp.dot(normed, qkv_full, preferred_element_type=jnp.float32)  25.5 us
    select_n x11, other arithmetic, advance(): stored = jnp.where(active, updated, stored)  21.6 us
  transfers between devices with their start and end apart: 35, of which 35 were waited for; matrix products, arithmetic and copies ran while one was open for 2% of the time, Pallas kernels for 0%

commit v1 on v0

v1 whole, which is shorter than its diff:
```python
import functools
import math

import jax
import jax.numpy as jnp
from jax import lax
from jax.experimental import pallas as pl
from jax.experimental.pallas import tpu as pltpu
from jax.sharding import PartitionSpec as P

HDIM = 128
WMAX = 64
MESH = pl.DeviceIdType.MESH
NY, NZ = 4, 8
STEP = ((0, 1), (0, -1), (1, 0), (-1, 0))
FLIP = (1, 0, 3, 2)
LAG = 4
BF = jnp.bfloat16
F32 = jnp.float32


def spread_trees():
    first, second = {}, {}
    for dz in range(1, NZ):
        first[0, dz] = second[0, dz] = 0 if dz <= 4 else 1
    for dz in range(NZ):
        first[1, dz], first[2, dz], first[3, dz] = 2, 2, 3
    second[1, 0], second[2, 0], second[3, 0] = 2, 2, 3
    for dy in range(1, NY):
        for dz in range(1, NZ):
            second[dy, dz] = 0 if dz <= 4 else 1
    second[1, 4], second[2, 4], second[3, 4], second[2, 5] = 2, 2, 3, 2

    def mirrored(tree):
        return {((-y) % NY, (-z) % NZ): FLIP[d] for (y, z), d in tree.items()}

    return [first, mirrored(first), second, mirrored(second)]


def before(offset, d):
    return ((offset[0] - STEP[d][0]) % NY, (offset[1] - STEP[d][1]) % NZ)


def spread_rounds():
    trees = spread_trees()
    kids = {}
    for part, tree in enumerate(trees):
        for offset, d in tree.items():
            kids.setdefault((part, before(offset, d)), []).append((part, offset))

    def height(node):
        return 1 + max([height(k) for k in kids.get(node, [])], default=0)

    def size(node):
        return 1 + sum(size(k) for k in kids.get(node, []))

    sent = {(part, (0, 0)): -LAG for part in range(4)}
    todo = {(part, offset): d for part, tree in enumerate(trees) for offset, d in tree.items()}
    rounds = []
    while todo:
        row = [None] * 4
        for d in range(4):
            ready = [
                n for n, way in todo.items()
                if way == d and sent.get((n[0], before(n[1], d)), 10**6) + LAG <= len(rounds)
            ]
            if ready:
                row[d] = max(ready, key=lambda n: (height(n), size(n)))
        for d in range(4):
            if row[d] is not None:
                sent[row[d]] = len(rounds)
                del todo[row[d]]
        rounds.append(row)
    return rounds


def kernel(
    frames, gain, w_qkv, w_out, lengths, windows, shifts, out,
    wall, xin, kbuf, vbuf, normed, qbuf, mixed, hid,
    own_sem, spread_send, spread_recv, frame_sem, halo_send, halo_recv, hop_send, hop_recv, out_sem,
):
    section = lax.axis_index("section")
    sections = lax.axis_size("section")
    tm = lax.axis_index("tm")
    tms = lax.axis_size("tm")
    y, z = tm // NZ, tm % NZ
    micros, rows, width = xin.shape
    heads_width = kbuf.shape[2]
    heads = heads_width // HDIM
    depth = w_qkv.shape[1]
    quarter = depth // 4
    scale = math.log2(math.e) / math.sqrt(HDIM)

    def at(dy, dz):
        return ((y + dy + NY) % NY) * NZ + (z + dz + NZ) % NZ

    own = [
        pltpu.make_async_copy(w_qkv.at[0, :, pl.ds(s * heads_width, heads_width)], wall.at[p, tm], own_sem.at[p])
        for p, s in ((0, 1), (1, 2), (2, 0))
    ]
    half = depth // 2
    for i in range(2):
        own.append(
            pltpu.make_async_copy(
                w_out.at[0, :, pl.ds(i * heads_width, heads_width)],
                wall.at[3, tm, pl.ds(i * half, half)], own_sem.at[3 + i],
            )
        )
    for c in own:
        c.start()
    frame_copy = pltpu.make_async_copy(frames, xin, frame_sem)

    @pl.when(section == 0)
    def _():
        frame_copy.start()

    barrier = pltpu.get_barrier_semaphore()
    for dy, dz in STEP:
        pl.semaphore_signal(barrier, inc=1, device_id=(section, at(dy, dz)), device_id_type=MESH)
    for d in (1, -1):
        pl.semaphore_signal(barrier, inc=1, device_id=(section, (tm + d + tms) % tms), device_id_type=MESH)
        pl.semaphore_signal(
            barrier, inc=1, device_id=((section + d + sections) % sections, tm), device_id_type=MESH
        )
    pl.semaphore_wait(barrier, 8)
    for c in own:
        c.wait()

    @pl.when(tm == 0)
    def _():
        for m in range(micros):
            kbuf[m, :WMAX, :] = jnp.zeros((WMAX, heads_width), BF)
            vbuf[m, :WMAX, :] = jnp.zeros((WMAX, heads_width), BF)

    @pl.when(tm == tms - 1)
    def _():
        for m in range(micros):
            kbuf[m, WMAX + rows:, :] = jnp.zeros((WMAX, heads_width), BF)
            vbuf[m, WMAX + rows:, :] = jnp.zeros((WMAX, heads_width), BF)

    rounds = spread_rounds()

    def slot(phase, part, offset):
        source = at(-offset[0], -offset[1])
        return wall.at[pl.ds(2 * phase, 2), source, pl.ds(part * quarter, quarter)]

    def spread_copy(phase, part, offset, d):
        block = slot(phase, part, offset)
        return pltpu.make_async_remote_copy(
            src_ref=block, dst_ref=block, send_sem=spread_send.at[phase],
            recv_sem=spread_recv.at[phase, part, ((offset[0] + STEP[d][0]) % NY) * NZ + (offset[1] + STEP[d][1]) % NZ],
            device_id=(section, at(*STEP[d])), device_id_type=MESH,
        )

    def spread_arrived(phase, part, offset):
        block = slot(phase, part, offset)
        pltpu.make_async_copy(block, block, spread_recv.at[phase, part, offset[0] * NZ + offset[1]]).wait()

    def spread(phase, _):
        seen = {(part, (0, 0)) for part in range(4)}
        for row in rounds:
            for d, node in enumerate(row):
                if node is None:
                    continue
                part, offset = node
                source = (part, before(offset, d))
                if source not in seen:
                    spread_arrived(phase, *source)
                    seen.add(source)
                spread_copy(phase, part, source[1], d).start()
        for part in range(4):
            for o in range(1, NY * NZ):
                node = (part, (o // NZ, o % NZ))
                if node not in seen:
                    spread_arrived(phase, *node)
        return 0

    lax.fori_loop(0, 2, spread, 0)
    for phase in range(2):
        sent = wall.at[pl.ds(2 * phase, 2), pl.ds(0, NY * NZ - 1)]
        pltpu.make_async_copy(sent, sent, spread_send.at[phase]).wait()

    window = windows[section]
    shift = shifts[section]

    def window_of(pos):
        n = pos - shift
        guess = jnp.floor((n.astype(F32) + 0.5) / window.astype(F32)).astype(jnp.int32)
        rest = n - guess * window
        return guess + (rest >= window).astype(jnp.int32) - (rest < 0).astype(jnp.int32)

    query_pos = tm * rows + lax.broadcasted_iota(jnp.int32, (rows, 1), 0)
    key_pos = tm * rows - WMAX + lax.broadcasted_iota(jnp.int32, (1, rows + 2 * WMAX), 1)
    total = rows * tms
    near = (window_of(query_pos) == window_of(key_pos)) & (key_pos >= 0) & (key_pos < total)
    same = query_pos == key_pos

    def halo(m, kind, side):
        buf = (kbuf, vbuf)[kind]
        src = (rows, WMAX)[side]
        dst = (0, WMAX + rows)[side]
        return pltpu.make_async_remote_copy(
            src_ref=buf.at[m, pl.ds(src, WMAX)], dst_ref=buf.at[m, pl.ds(dst, WMAX)],
            send_sem=halo_send.at[m, kind, side], recv_sem=halo_recv.at[m, kind, side],
            device_id=(section, (tm + (1, -1)[side] + tms) % tms), device_id_type=MESH,
        )

    def halo_start(m, kind):
        @pl.when(tm < tms - 1)
        def _():
            halo(m, kind, 0).start()

        @pl.when(tm > 0)
        def _():
            halo(m, kind, 1).start()

    def halo_arrived(m, kind):
        @pl.when(tm > 0)
        def _():
            halo(m, kind, 0).wait_recv()

        @pl.when(tm < tms - 1)
        def _():
            halo(m, kind, 1).wait_recv()

    chunk = heads_width // 2
    chunks = width // chunk

    def hop(m, c):
        return pltpu.make_async_remote_copy(
            src_ref=hid.at[m, :, pl.ds(c * chunk, chunk)], dst_ref=xin.at[m, :, pl.ds(c * chunk, chunk)],
            send_sem=hop_send.at[m, c], recv_sem=hop_recv.at[m, c],
            device_id=((section + 1) % sections, tm), device_id_type=MESH,
        )

    @pl.when(section == 0)
    def _():
        frame_copy.wait()

    def project(slab, col):
        w = wall[slab, :, :, col:col + chunk].reshape(width, chunk)
        return jnp.dot(normed[...], w, preferred_element_type=F32).astype(BF)

    def stage(m, _):
        @pl.when(section > 0)
        def _():
            for c in range(chunks):
                hop(m, c).wait_recv()

        x = xin[m].astype(F32)
        centered = x - jnp.mean(x, axis=-1, keepdims=True)
        variance = jnp.mean(centered * centered, axis=-1, keepdims=True)
        normed[...] = (centered * lax.rsqrt(variance + 1e-05) * gain[...].astype(F32)).astype(BF)
        for kind, buf in enumerate((kbuf, vbuf)):
            for col in range(0, heads_width, chunk):
                buf[m, WMAX:WMAX + rows, col:col + chunk] = project(kind, col)
            halo_start(m, kind)
        for col in range(0, heads_width, chunk):
            qbuf[:, col:col + chunk] = project(2, col)
        length = lengths[m, 0]
        allowed = near & ((key_pos < length) | same)
        halo_arrived(m, 0)
        halo_arrived(m, 1)
        for h in range(heads):
            cols = slice(h * HDIM, (h + 1) * HDIM)
            scores = lax.dot_general(
                qbuf[:, cols], kbuf[m, :, cols], (((1,), (1,)), ((), ())), preferred_element_type=F32
            )
            scores = jnp.where(allowed, scores, -1e30)
            weights = jnp.exp2((scores - jnp.max(scores, axis=-1, keepdims=True)) * scale)
            total_weight = jnp.sum(weights, axis=-1, keepdims=True)
            head = jnp.dot(weights.astype(BF), vbuf[m, :, cols], preferred_element_type=F32)
            mixed[:, cols] = (head / total_weight).astype(BF)
        valid = (query_pos < length).astype(F32)
        for c in range(chunks):
            part, col = c * chunk // heads_width, c * chunk % heads_width
            w = wall[3, :, part * half:(part + 1) * half, col:col + chunk].reshape(heads_width, chunk)
            projection = jnp.dot(mixed[...], w, preferred_element_type=F32)
            cols = slice(c * chunk, (c + 1) * chunk)
            hid[m, :, cols] = (xin[m, :, cols].astype(F32) + valid * projection).astype(BF)

            @pl.when(section < sections - 1)
            def _():
                hop(m, c).start()

        pltpu.make_async_copy(hid.at[m], out.at[0, m], out_sem.at[m]).start()
        return 0

    lax.fori_loop(0, micros, stage, 0)

    def finish(m, _):
        pltpu.make_async_copy(hid.at[m], out.at[0, m], out_sem.at[m]).wait()
        for kind in range(2):
            @pl.when(tm < tms - 1)
            def _():
                halo(m, kind, 0).wait_send()

            @pl.when(tm > 0)
            def _():
                halo(m, kind, 1).wait_send()

        @pl.when(section < sections - 1)
        def _():
            for c in range(chunks):
                hop(m, c).wait_send()

        return 0

    lax.fori_loop(0, micros, finish, 0)


def on_device(frames, norm_gain, w_qkv, w_out, lengths, windows, shifts):
    micros, rows, width = frames.shape
    depth = w_qkv.shape[1]
    heads_width = w_qkv.shape[2] // 3
    tms = lax.axis_size("tm")
    dma = pltpu.SemaphoreType.DMA
    vmem = pl.BlockSpec(memory_space=pltpu.VMEM)
    smem = pl.BlockSpec(memory_space=pltpu.SMEM)
    hbm = pl.BlockSpec(memory_space=pl.ANY)
    keys = rows + 2 * WMAX
    return pl.pallas_call(
        kernel,
        out_shape=jax.ShapeDtypeStruct((1, micros, rows, width), BF),
        in_specs=[hbm, vmem, hbm, hbm, smem, smem, smem],
        out_specs=hbm,
        scratch_shapes=[
            pltpu.VMEM((4, tms, depth, heads_width), BF),
            pltpu.VMEM((micros, rows, width), BF),
            pltpu.VMEM((micros, keys, heads_width), BF),
            pltpu.VMEM((micros, keys, heads_width), BF),
            pltpu.VMEM((rows, width), BF),
            pltpu.VMEM((rows, heads_width), BF),
            pltpu.VMEM((rows, heads_width), BF),
            pltpu.VMEM((micros, rows, width), BF),
            dma((5,)), dma((2,)), dma((2, 4, tms)), dma,
            dma((micros, 2, 2)), dma((micros, 2, 2)), dma((micros, 4)), dma((micros, 4)), dma((micros,)),
        ],
        compiler_params=pltpu.CompilerParams(
            collective_id=0, has_side_effects=True, vmem_limit_bytes=52 << 20
        ),
        name="relay",
    )(frames, norm_gain, w_qkv, w_out, lengths, windows, shifts)


def solution(mesh):
    return jax.shard_map(
        on_device,
        mesh=mesh,
        in_specs=(
            P(None, "tm", None),
            P("section", None),
            P("section", "tm", None),
            P("section", "tm", None),
            P(),
            P(),
            P(),
        ),
        out_specs=P("section", None, "tm", None),
        check_vma=False,
    )
```

time: 817 us -> 248 us (0.30)
  waiting for transfers between devices: 495 us -> 0 us
  Pallas kernels: 0 us -> 240 us
  starting transfers between devices: 103 us -> 0 us
  other arithmetic: 82.9 us -> 0 us
  local copies, waits for them, and re-layouts: 62.4 us -> 7.8 us
  matrix products: 52.9 us -> 0 us
  between operations: 13.4 us -> 0.01 us
    ppermute x33 -> x0, waiting for transfers between devices: 292 us -> none  [the longest x11 238 us: from_behind(): return lax.ppermute(block, axis, route)]
    pallas_call x0 -> x1, Pallas kernels: none -> 240 us  [on_device(): pl.pallas_call(kernel, out_shape=jax.ShapeDtypeStruct((1, micros, rows, w...]
    all_gather x2 -> x0, waiting for transfers between devices: 201 us -> none  [the longest x1 122 us: on_device(): lax.all_gather(w_qkv[0], 'tm', axis=0, tiled=True)]
    ppermute x33 -> x0, starting transfers between devices: 103 us -> none  [the longest x11 67.5 us: extended(): lax.ppermute(head, axis, [((i + 1) % count, i) for i in range(ends)])]
    dot_general x16 -> x0, matrix products: 50.3 us -> none  [the longest x4 25.5 us: apply_layer(): jnp.dot(normed, qkv_full, preferred_element_type=jnp.float32)]
    while x55 -> x0, local copies, waits for them, and re-layouts: 42.3 us -> none
    select_n x19 -> x0, other arithmetic: 33 us -> none  [the longest x11 21.6 us: advance(): stored = jnp.where(active, updated, stored)]
    concatenate x11 -> x0, other arithmetic: 21.5 us -> none  [extended(): jnp.concatenate([lax.ppermute(tail, axis, [(i, (i + 1) % count) for i in...]
  transfers between devices with their start and end apart: 35 -> 0, of which waited for: 35 -> 0; matrix products, arithmetic and copies ran while one was open for 2% -> 0% of each run, Pallas kernels for 0% -> 0%
where the time goes in v1:
time: 248 us
  Pallas kernels  240 us (97%)
  local copies, waits for them, and re-layouts  7.8 us (3%)
    pallas_call x1, Pallas kernels, on_device(): pl.pallas_call(kernel, out_shape=jax.ShapeDtypeStruct((1, micros, rows, w...  240 us
    unnamed x12, local copies, waits for them, and re-layouts  7.8 us

profile of v1, /device:TPU:15, one launch (start us, length us, event | category | flops | bytes accessed | tf_op | source)
XLA Modules:
  0.0 247.9 jit_solution(5561423069023739120)
XLA Ops:
  0.0 0.7 copy.8.lengths
  0.7 0.0 copy-start
  0.7 1.0 copy-done
  1.7 0.0 copy-start.1
  1.7 0.9 copy-done.1
  2.6 0.0 copy-start.2
  2.6 0.7 copy-done.2
  3.3 0.0 copy-start.3
  3.3 0.7 copy-done.3
  4.0 0.0 copy-start.4
  4.0 0.7 copy-done.4
  4.7 240.1 %relay.1 = bf16[1,4,128,2048]{3,2,1,0:T(8,128)(2,1)} custom-call(bf16[4,128,2048]{2,1,0:T(8,128)(2,1)} %frames.1, bf16[1,2048]{1,0:T(2,128)(2,1)S(1)} %copy-done.2, bf16[1,64,3072]{2,1,0:T(8,128)(2,1)S(1)} %copy-done, bf16[1,32,2048]{2,1,0:T(8,128)(2,1)S(1)} %copy-done.1, s32[4,1]{1,0:T(4,128)S(1)} %copy.8.lengths, s32[8]{0:T(128)S(1)} %copy-done.3, ...), custom_call_target="tpu_custom_call" | custom-call | tf_op jit(solution)/shard_map/relay/pallas_call | solution.py:322
  244.8 3.2 %copy.10 = bf16[1,4,128,2048]{3,2,1,0:T(8,128)(2,1)} copy(bf16[1,4,128,2048]{3,2,1,0:T(8,128)(2,1)} %relay.1) | data formatting | bytes 4194304
Async XLA Ops:
  0.7 1.0 copy-start
  1.7 0.9 copy-start.1
  2.6 0.7 copy-start.2
  3.3 0.7 copy-start.3
  4.0 0.7 copy-start.4

commit v2 on v1

v2 whole, which is shorter than its diff:
```python
import functools
import math

import jax
import jax.numpy as jnp
from jax import lax
from jax.experimental import pallas as pl
from jax.experimental.pallas import tpu as pltpu
from jax.sharding import PartitionSpec as P

HDIM = 128
WMAX = 64
MESH = pl.DeviceIdType.MESH
NY, NZ = 4, 8
STEP = ((0, 1), (0, -1), (1, 0), (-1, 0))
FLIP = (1, 0, 3, 2)
LAG = 5
GROUP = 2 * HDIM
LENT = 3 * HDIM
BF = jnp.bfloat16
F32 = jnp.float32


def spread_trees():
    first, second = {}, {}
    for dz in range(1, NZ):
        first[0, dz] = second[0, dz] = 0 if dz <= 4 else 1
    for dz in range(NZ):
        first[1, dz], first[2, dz], first[3, dz] = 2, 2, 3
    second[1, 0], second[2, 0], second[3, 0] = 2, 2, 3
    for dy in range(1, NY):
        for dz in range(1, NZ):
            second[dy, dz] = 0 if dz <= 4 else 1
    second[1, 4], second[2, 4], second[3, 4], second[2, 5] = 2, 2, 3, 2

    def mirrored(tree):
        return {((-y) % NY, (-z) % NZ): FLIP[d] for (y, z), d in tree.items()}

    return [first, mirrored(first), second, mirrored(second)]


def before(offset, d):
    return ((offset[0] - STEP[d][0]) % NY, (offset[1] - STEP[d][1]) % NZ)


def spread_rounds():
    trees = spread_trees()
    kids = {}
    for part, tree in enumerate(trees):
        for offset, d in tree.items():
            kids.setdefault((part, before(offset, d)), []).append((part, offset))

    def height(node):
        return 1 + max([height(k) for k in kids.get(node, [])], default=0)

    def size(node):
        return 1 + sum(size(k) for k in kids.get(node, []))

    sent = {(part, (0, 0)): -LAG for part in range(4)}
    todo = {(part, offset): d for part, tree in enumerate(trees) for offset, d in tree.items()}
    rounds = []
    while todo:
        row = [None] * 4
        for d in range(4):
            ready = [
                n for n, way in todo.items()
                if way == d and sent.get((n[0], before(n[1], d)), 10**6) + LAG <= len(rounds)
            ]
            if ready:
                row[d] = max(ready, key=lambda n: (height(n), size(n)))
        for d in range(4):
            if row[d] is not None:
                sent[row[d]] = len(rounds)
                del todo[row[d]]
        rounds.append(row)
    return rounds


def kernel(
    frames, gain_hbm, w_qkv, w_out, lengths_hbm, windows_hbm, shifts_hbm, out,
    wall, lent, xin, kv, normed, qbuf, mixed, hid, gain, lengths, windows, shifts,
    own_sem, small_sem, spread_send, spread_recv, lend_sem, lent_send, lent_recv, frame_sem, halo_send, halo_recv, hop_send, hop_recv,
    out_sem,
):
    section = lax.axis_index("section")
    sections = lax.axis_size("section")
    tm = lax.axis_index("tm")
    tms = lax.axis_size("tm")
    y, z = tm // NZ, tm % NZ
    micros, rows, width = xin.shape
    heads_width = wall.shape[3]
    groups = heads_width // GROUP
    depth = w_qkv.shape[1]
    quarter, half = depth // 4, depth // 2
    pair = 2 * GROUP
    pairs = heads_width // pair
    scale = math.log2(math.e) / math.sqrt(HDIM)

    def at(dy, dz):
        return ((y + dy + NY) % NY) * NZ + (z + dz + NZ) % NZ

    own = []

    def take(source, target):
        own.append(pltpu.make_async_copy(source, target, own_sem.at[len(own)]))

    for g in range(groups):
        for kind in range(2):
            take(
                w_qkv.at[0, :, pl.ds((1 + kind) * heads_width + g * GROUP, GROUP)],
                wall.at[g // pairs, tm, :, pl.ds(g % pairs * pair + kind * GROUP, GROUP)],
            )
    take(w_qkv.at[0, :, pl.ds(0, heads_width)], wall.at[2, tm])
    for i in range(2):
        take(w_out.at[0, :, pl.ds(i * heads_width, heads_width)], wall.at[3, tm, pl.ds(i * half, half)])
    small = [
        pltpu.make_async_copy(source, target, small_sem.at[i])
        for i, (source, target) in enumerate(
            ((gain_hbm, gain), (lengths_hbm, lengths), (windows_hbm, windows), (shifts_hbm, shifts))
        )
    ]
    for c in own + small:
        c.start()
    frame_copy = pltpu.make_async_copy(frames, xin, frame_sem)

    @pl.when(section == 0)
    def _():
        frame_copy.start()

    barrier = pltpu.get_barrier_semaphore()
    for dy, dz in STEP:
        pl.semaphore_signal(barrier, inc=1, device_id=(section, at(dy, dz)), device_id_type=MESH)
    for d in (1, -1):
        pl.semaphore_signal(barrier, inc=1, device_id=(section, (tm + d + tms) % tms), device_id_type=MESH)
    for d in (1, -1, 2, -2):
        pl.semaphore_signal(
            barrier, inc=1, device_id=((section + d + sections) % sections, tm), device_id_type=MESH
        )

    @pl.when(tm == 0)
    def _():
        for m in range(micros):
            kv[m, :WMAX, :] = jnp.zeros((WMAX, 2 * heads_width), BF)

    @pl.when(tm == tms - 1)
    def _():
        for m in range(micros):
            kv[m, WMAX + rows:, :] = jnp.zeros((WMAX, 2 * heads_width), BF)

    borrows, lends = section < 2, section >= sections - 2

    for c in small + own:
        c.wait()
    pl.semaphore_wait(barrier, 10)

    @pl.when(section == 0)
    def _():
        frame_copy.wait()

    window = windows[section]
    shift = shifts[section]

    def window_of(pos):
        n = pos - shift
        guess = jnp.floor((n.astype(F32) + 0.5) / window.astype(F32)).astype(jnp.int32)
        rest = n - guess * window
        return guess + (rest >= window).astype(jnp.int32) - (rest < 0).astype(jnp.int32)

    query_pos = tm * rows + lax.broadcasted_iota(jnp.int32, (rows, 1), 0)
    key_pos = tm * rows - WMAX + lax.broadcasted_iota(jnp.int32, (1, rows + 2 * WMAX), 1)
    same = query_pos == key_pos

    def halo(m, g, side):
        src = (rows, WMAX)[side]
        dst = (0, WMAX + rows)[side]
        return pltpu.make_async_remote_copy(
            src_ref=kv.at[m, pl.ds(src, WMAX), pl.ds(g * pair, pair)],
            dst_ref=kv.at[m, pl.ds(dst, WMAX), pl.ds(g * pair, pair)],
            send_sem=halo_send.at[m, g, side], recv_sem=halo_recv.at[m, g, side],
            device_id=(section, (tm + (1, -1)[side] + tms) % tms), device_id_type=MESH,
        )

    def each_side(act, before_me, after_me):
        @pl.when(tm < tms - 1)
        def _():
            act(after_me)

        @pl.when(tm > 0)
        def _():
            act(before_me)

    chunk = heads_width // 2
    chunks = width // chunk

    def hop(m, c):
        return pltpu.make_async_remote_copy(
            src_ref=hid.at[m, :, pl.ds(c * chunk, chunk)], dst_ref=xin.at[m, :, pl.ds(c * chunk, chunk)],
            send_sem=hop_send.at[m, c], recv_sem=hop_recv.at[m, c],
            device_id=((section + 1) % sections, tm), device_id_type=MESH,
        )

    def project(slab, col):
        w = wall[slab, :, :, col:col + pair].reshape(width, pair)
        return jnp.dot(normed[...], w, preferred_element_type=F32).astype(BF)

    def enter(m):
        @pl.when(section > 0)
        def _():
            for c in range(chunks):
                hop(m, c).wait_recv()

        x = xin[m].astype(F32)
        centered = x - jnp.mean(x, axis=-1, keepdims=True)
        variance = jnp.mean(centered * centered, axis=-1, keepdims=True)
        normed[...] = (centered * lax.rsqrt(variance + 1e-05) * gain[...].astype(F32)).astype(BF)

    def keys_values(m, slab, i):
        g = slab * pairs + i
        cols = pl.ds(pl.multiple_of(g * pair, pair), pair)
        kv[m, pl.ds(WMAX, rows), cols] = project(slab, i * pair)
        each_side(lambda side: halo(m, g, side).start(), 1, 0)

    rounds = spread_rounds()
    near_cols = heads_width - LENT
    lent_cols = pl.ds(near_cols, LENT)

    def blocks(phase, source, first, count):
        line = pl.ds(first, count)
        if phase == 0:
            return wall.at[pl.ds(0, 2), source, line]
        if phase == 1:
            return wall.at[pl.ds(2, 2), source, line, pl.ds(0, near_cols)]
        if phase == 2:
            return wall.at[pl.ds(2, 2), source, line, lent_cols]
        return lent.at[:, source, line]

    def slot(phase, part, offset):
        return blocks(phase, at(-offset[0], -offset[1]), part * quarter, quarter)

    def spread_copy(phase, part, offset, d):
        block = slot(phase, part, offset)
        return pltpu.make_async_remote_copy(
            src_ref=block, dst_ref=block, send_sem=spread_send.at[phase],
            recv_sem=spread_recv.at[phase, part, ((offset[0] + STEP[d][0]) % NY) * NZ + (offset[1] + STEP[d][1]) % NZ],
            device_id=(section, at(*STEP[d])), device_id_type=MESH,
        )

    def lend():
        return pltpu.make_async_remote_copy(
            src_ref=blocks(2, tm, 0, depth), dst_ref=blocks(3, tm, 0, depth), send_sem=lend_sem.at[0],
            recv_sem=lend_sem.at[1], device_id=((section + sections - 2) % sections, tm), device_id_type=MESH,
        )

    def spread_arrived(phase, part, offset):
        block = slot(phase, part, offset)
        pltpu.make_async_copy(block, block, spread_recv.at[phase, part, offset[0] * NZ + offset[1]]).wait()
        if phase == 3:
            pltpu.make_async_remote_copy(
                src_ref=block, dst_ref=slot(2, part, offset), send_sem=lent_send, recv_sem=lent_recv,
                device_id=((section + 2) % sections, tm), device_id_type=MESH,
            ).start()

    def spread(phase, behind=()):
        seen = {(part, (0, 0)) for part in range(4)}
        for r, row in enumerate(rounds):
            if r == LAG:
                for node in behind:
                    spread_arrived(*node)
            for d, node in enumerate(row):
                if node is None:
                    continue
                part, source = node[0], before(node[1], d)
                if (part, source) not in seen:
                    spread_arrived(phase, part, source)
                    seen.add((part, source))
                spread_copy(phase, part, source, d).start()
        every = [(part, (o // NZ, o % NZ)) for part in range(4) for o in range(1, NY * NZ)]
        return [(phase, *node) for node in every if node not in seen]

    def spread_sent(phase):
        if phase == 3:
            sent = lent.at[:, pl.ds(0, NY * NZ - 1)]
        elif phase == 0:
            sent = wall.at[pl.ds(0, 2), pl.ds(0, NY * NZ - 1)]
        else:
            sent = wall.at[pl.ds(2, 2), pl.ds(0, NY * NZ - 1), :, pl.ds(0, near_cols) if phase == 1 else lent_cols]
        return sent

    def all_sent(phase):
        sent = spread_sent(phase)
        pltpu.make_async_copy(sent, sent, spread_send.at[phase]).wait()

    @pl.when(borrows)
    def _():
        lend().start()

    @pl.when(lends)
    def _():
        lend().wait_recv()
        for node in spread(3):
            spread_arrived(*node)

    for node in spread(1, spread(0)):
        spread_arrived(*node)

    @pl.when(borrows)
    def _():
        lend().wait_send()
        sent = spread_sent(2)
        pltpu.make_async_copy(sent, sent, lent_recv).wait()

    @pl.when(section >= 2)
    def _():
        for node in spread(2):
            spread_arrived(*node)

    def queries(m):
        for col in range(0, heads_width, pair):
            qbuf[m, :, col:col + pair] = project(2, col)

    def attend(m):
        length = lengths[m, 0]
        near = (window_of(query_pos) == window_of(key_pos)) & (key_pos >= 0) & (key_pos < rows * tms)
        allowed = near & ((key_pos < length) | same)
        valid = (query_pos < length).astype(F32)
        for h in range(heads_width // HDIM):
            qcol = h * HDIM
            if qcol % (heads_width // 2) == 0:
                for g in range(qcol // GROUP, (qcol + heads_width // 2) // GROUP):
                    each_side(lambda side: halo(m, g, side).wait_recv(), 0, 1)
            kcol = qcol // GROUP * pair + qcol % GROUP
            vcol = kcol + GROUP
            scores = lax.dot_general(
                qbuf[m, :, qcol:qcol + HDIM], kv[m, :, kcol:kcol + HDIM], (((1,), (1,)), ((), ())),
                preferred_element_type=F32,
            )
            scores = jnp.where(allowed, scores, -1e30)
            weights = jnp.exp2((scores - jnp.max(scores, axis=-1, keepdims=True)) * scale)
            total_weight = jnp.sum(weights, axis=-1, keepdims=True)
            head = jnp.dot(weights.astype(BF), kv[m, :, vcol:vcol + HDIM], preferred_element_type=F32)
            mixed[:, qcol:qcol + HDIM] = (head / total_weight).astype(BF)
        for c in range(chunks):
            part, col = c * chunk // heads_width, c * chunk % heads_width
            w = wall[3, :, part * half:(part + 1) * half, col:col + chunk].reshape(heads_width, chunk)
            cols = slice(c * chunk, (c + 1) * chunk)
            projection = jnp.dot(mixed[...], w, preferred_element_type=F32)
            hid[m, :, cols] = (xin[m, :, cols].astype(F32) + valid * projection).astype(BF)

            @pl.when(section < sections - 1)
            def _():
                hop(m, c).start()

        pltpu.make_async_copy(hid.at[m], out.at[0, m], out_sem.at[m]).start()

    def stage(i, _):
        @pl.when(i < micros)
        def _():
            enter(i)
            for slab in range(2):
                for j in range(pairs):
                    keys_values(i, slab, j)
            queries(i)

        @pl.when(i > 0)
        def _():
            attend(i - 1)

        return 0

    lax.fori_loop(0, micros + 1, stage, 0)

    for phase in range(2):
        all_sent(phase)

    @pl.when(section >= 2)
    def _():
        all_sent(2)

    @pl.when(lends)
    def _():
        all_sent(3)
        sent = spread_sent(3)
        pltpu.make_async_copy(sent, sent, lent_send).wait()

    def finish(m, _):
        pltpu.make_async_copy(hid.at[m], out.at[0, m], out_sem.at[m]).wait()
        for g in range(groups):
            each_side(lambda side: halo(m, g, side).wait_send(), 1, 0)

        @pl.when(section < sections - 1)
        def _():
            for c in range(chunks):
                hop(m, c).wait_send()

        return 0

    lax.fori_loop(0, micros, finish, 0)


def on_device(frames, norm_gain, w_qkv, w_out, lengths, windows, shifts):
    micros, rows, width = frames.shape
    depth = w_qkv.shape[1]
    heads_width = w_qkv.shape[2] // 3
    groups = heads_width // GROUP
    tms = lax.axis_size("tm")
    dma = pltpu.SemaphoreType.DMA
    hbm = pl.BlockSpec(memory_space=pl.ANY)
    return pl.pallas_call(
        kernel,
        out_shape=jax.ShapeDtypeStruct((1, micros, rows, width), BF),
        in_specs=[hbm] * 7,
        out_specs=hbm,
        scratch_shapes=[
            pltpu.VMEM((4, tms, depth, heads_width), BF),
            pltpu.VMEM((2, tms, depth, LENT), BF),
            pltpu.VMEM((micros, rows, width), BF),
            pltpu.VMEM((micros, rows + 2 * WMAX, 2 * heads_width), BF),
            pltpu.VMEM((rows, width), BF),
            pltpu.VMEM((micros, rows, heads_width), BF),
            pltpu.VMEM((rows, heads_width), BF),
            pltpu.VMEM((micros, rows, width), BF),
            pltpu.VMEM(norm_gain.shape, BF),
            pltpu.SMEM(lengths.shape, jnp.int32),
            pltpu.SMEM(windows.shape, jnp.int32),
            pltpu.SMEM(shifts.shape, jnp.int32),
            dma((2 * groups + 3,)), dma((4,)), dma((4,)), dma((4, 4, tms)), dma((2,)), dma, dma, dma,
            dma((micros, groups, 2)), dma((micros, groups, 2)), dma((micros, 4)), dma((micros, 4)), dma((micros,)),
        ],
        compiler_params=pltpu.CompilerParams(
            collective_id=0, has_side_effects=True, vmem_limit_bytes=52 << 20
        ),
        name="relay",
    )(frames, norm_gain, w_qkv, w_out, lengths, windows, shifts)


def solution(mesh):
    return jax.shard_map(
        on_device,
        mesh=mesh,
        in_specs=(
            P(None, "tm", None),
            P("section", None),
            P("section", "tm", None),
            P("section", "tm", None),
            P(),
            P(),
            P(),
        ),
        out_specs=P("section", None, "tm", None),
        check_vma=False,
    )
```

time: 248 us -> 220 us (0.89)
  Pallas kernels: 240 us -> 212 us
    pallas_call x1, Pallas kernels: 240 us -> 212 us  [on_device(): pl.pallas_call(kernel, out_shape=jax.ShapeDtypeStruct((1, micros, rows, w...]
where the time goes in v2:
time: 220 us; the launch traced here: 219 us
  Pallas kernels  212 us (96%)
  local copies, waits for them, and re-layouts  7.8 us (4%)
    pallas_call x1, Pallas kernels, on_device(): pl.pallas_call(kernel, out_shape=jax.ShapeDtypeStruct((1, micros, rows, w...  212 us
    unnamed x12, local copies, waits for them, and re-layouts  7.8 us

profile of v2, /device:TPU:15, one launch (start us, length us, event | category | flops | bytes accessed | tf_op | source)
XLA Modules:
  0.0 219.5 jit_solution(16969324907721508242)
XLA Ops:
  0.0 0.7 copy.8.lengths_hbm
  0.7 0.0 copy-start
  0.7 1.0 copy-done
  1.7 0.0 copy-start.1
  1.7 0.9 copy-done.1
  2.6 0.0 copy-start.2
  2.6 0.7 copy-done.2
  3.3 0.0 copy-start.3
  3.3 0.7 copy-done.3
  4.0 0.0 copy-start.4
  4.0 0.7 copy-done.4
  4.7 211.7 %relay.1 = bf16[1,4,128,2048]{3,2,1,0:T(8,128)(2,1)} custom-call(bf16[4,128,2048]{2,1,0:T(8,128)(2,1)} %frames.1, bf16[1,2048]{1,0:T(2,128)(2,1)S(1)} %copy-done.2, bf16[1,64,3072]{2,1,0:T(8,128)(2,1)S(1)} %copy-done, bf16[1,32,2048]{2,1,0:T(8,128)(2,1)S(1)} %copy-done.1, s32[4,1]{1,0:T(4,128)S(1)} %copy.8.lengths_hbm, s32[8]{0:T(128)S(1)} %copy-done.3, ...), custom_call_target="tpu_custom_call" | custom-call | tf_op jit(solution)/shard_map/relay/pallas_call | solution.py:408
  216.3 3.2 %copy.10 = bf16[1,4,128,2048]{3,2,1,0:T(8,128)(2,1)} copy(bf16[1,4,128,2048]{3,2,1,0:T(8,128)(2,1)} %relay.1) | data formatting | bytes 4194304
Async XLA Ops:
  0.7 1.0 copy-start
  1.7 0.9 copy-start.1
  2.6 0.7 copy-start.2
  3.3 0.7 copy-start.3
  4.0 0.7 copy-start.4

commit v3 on v2

--- a/solution.py
+++ b/solution.py
@@ -319,7 +319,7 @@
             qbuf[m, :, col:col + pair] = project(2, col)
 
     def attend(m):
-        length = lengths[m, 0]
+        length = lengths[m]
         near = (window_of(query_pos) == window_of(key_pos)) & (key_pos >= 0) & (key_pos < rows * tms)
         allowed = near & ((key_pos < length) | same)
         valid = (query_pos < length).astype(F32)
@@ -359,11 +359,14 @@
             for slab in range(2):
                 for j in range(pairs):
                     keys_values(i, slab, j)
+
+        @pl.when(i > 0)
+        def _():
+            attend(i - 1)
+
+        @pl.when(i < micros)
+        def _():
             queries(i)
-
-        @pl.when(i > 0)
-        def _():
-            attend(i - 1)
 
         return 0
 
@@ -404,7 +407,7 @@
     groups = heads_width // GROUP
     tms = lax.axis_size("tm")
     dma = pltpu.SemaphoreType.DMA
-    hbm = pl.BlockSpec(memory_space=pl.ANY)
+    hbm = pl.BlockSpec(memory_space=pltpu.HBM)
     return pl.pallas_call(
         kernel,
         out_shape=jax.ShapeDtypeStruct((1, micros, rows, width), BF),
@@ -420,17 +423,17 @@
             pltpu.VMEM((rows, heads_width), BF),
             pltpu.VMEM((micros, rows, width), BF),
             pltpu.VMEM(norm_gain.shape, BF),
-            pltpu.SMEM(lengths.shape, jnp.int32),
+            pltpu.SMEM((micros,), jnp.int32),
             pltpu.SMEM(windows.shape, jnp.int32),
             pltpu.SMEM(shifts.shape, jnp.int32),
             dma((2 * groups + 3,)), dma((4,)), dma((4,)), dma((4, 4, tms)), dma((2,)), dma, dma, dma,
             dma((micros, groups, 2)), dma((micros, groups, 2)), dma((micros, 4)), dma((micros, 4)), dma((micros,)),
         ],
         compiler_params=pltpu.CompilerParams(
-            collective_id=0, has_side_effects=True, vmem_limit_bytes=52 << 20
+            collective_id=0, has_side_effects=True, vmem_limit_bytes=60 << 20
         ),
         name="relay",
-    )(frames, norm_gain, w_qkv, w_out, lengths, windows, shifts)
+    )(frames, norm_gain, w_qkv, w_out, lengths.reshape(micros), windows, shifts)
 
 
 def solution(mesh):

time: 220 us -> 213 us (0.968)
  local copies, waits for them, and re-layouts: 7.8 us -> 3.16 us
    unnamed x12 -> x1, local copies, waits for them, and re-layouts: 7.8 us -> 3.16 us
where the time goes in v3:
time: 213 us
  Pallas kernels  210 us (99%)
  local copies, waits for them, and re-layouts  3.16 us (1%)
    pallas_call x1, Pallas kernels, on_device(): pl.pallas_call(kernel, out_shape=jax.ShapeDtypeStruct((1, micros, rows, w...  210 us

profile of v3, /device:TPU:15, one launch (start us, length us, event | category | flops | bytes accessed | tf_op | source)
XLA Modules:
  0.0 213.3 jit_solution(13148144765115722502)
XLA Ops:
  0.0 210.1 %relay.1 = bf16[1,4,128,2048]{3,2,1,0:T(8,128)(2,1)} custom-call(bf16[4,128,2048]{2,1,0:T(8,128)(2,1)} %frames.1, bf16[1,2048]{1,0:T(2,128)(2,1)} %gain_hbm.1, bf16[1,64,3072]{2,1,0:T(8,128)(2,1)} %w_qkv.1, bf16[1,32,2048]{2,1,0:T(8,128)(2,1)} %w_out.1, s32[4]{0:T(128)} %bitcast.1, s32[8]{0:T(128)} %windows_hbm.1, s32[8]{0:T(128)} %shifts_hbm.1), custom_call_target="tpu_custom_call" | custom-call | tf_op jit(solution)/shard_map/relay/pallas_call | solution.py:411
  210.1 3.2 %copy.9 = bf16[1,4,128,2048]{3,2,1,0:T(8,128)(2,1)} copy(bf16[1,4,128,2048]{3,2,1,0:T(8,128)(2,1)} %relay.1) | data formatting | bytes 4194304

commit v4 on v3

--- a/solution.py
+++ b/solution.py
@@ -14,8 +14,8 @@
 NY, NZ = 4, 8
 STEP = ((0, 1), (0, -1), (1, 0), (-1, 0))
 FLIP = (1, 0, 3, 2)
-LAG = 5
-GROUP = 2 * HDIM
+LAG = 6
+GROUP = 4 * HDIM
 LENT = 3 * HDIM
 BF = jnp.bfloat16
 F32 = jnp.float32
@@ -78,7 +78,7 @@
 
 def kernel(
     frames, gain_hbm, w_qkv, w_out, lengths_hbm, windows_hbm, shifts_hbm, out,
-    wall, lent, xin, kv, normed, qbuf, mixed, hid, gain, lengths, windows, shifts,
+    wall, lent, xin, kv, normed, qbuf, mixed, total, hid, gain, lengths, windows, shifts,
     own_sem, small_sem, spread_send, spread_recv, lend_sem, lent_send, lent_recv, frame_sem, halo_send, halo_recv, hop_send, hop_recv,
     out_sem,
 ):
@@ -323,32 +323,36 @@
         near = (window_of(query_pos) == window_of(key_pos)) & (key_pos >= 0) & (key_pos < rows * tms)
         allowed = near & ((key_pos < length) | same)
         valid = (query_pos < length).astype(F32)
-        for h in range(heads_width // HDIM):
-            qcol = h * HDIM
-            if qcol % (heads_width // 2) == 0:
-                for g in range(qcol // GROUP, (qcol + heads_width // 2) // GROUP):
-                    each_side(lambda side: halo(m, g, side).wait_recv(), 0, 1)
-            kcol = qcol // GROUP * pair + qcol % GROUP
-            vcol = kcol + GROUP
-            scores = lax.dot_general(
-                qbuf[m, :, qcol:qcol + HDIM], kv[m, :, kcol:kcol + HDIM], (((1,), (1,)), ((), ())),
-                preferred_element_type=F32,
-            )
-            scores = jnp.where(allowed, scores, -1e30)
-            weights = jnp.exp2((scores - jnp.max(scores, axis=-1, keepdims=True)) * scale)
-            total_weight = jnp.sum(weights, axis=-1, keepdims=True)
-            head = jnp.dot(weights.astype(BF), kv[m, :, vcol:vcol + HDIM], preferred_element_type=F32)
-            mixed[:, qcol:qcol + HDIM] = (head / total_weight).astype(BF)
-        for c in range(chunks):
-            part, col = c * chunk // heads_width, c * chunk % heads_width
-            w = wall[3, :, part * half:(part + 1) * half, col:col + chunk].reshape(heads_width, chunk)
-            cols = slice(c * chunk, (c + 1) * chunk)
-            projection = jnp.dot(mixed[...], w, preferred_element_type=F32)
-            hid[m, :, cols] = (xin[m, :, cols].astype(F32) + valid * projection).astype(BF)
-
-            @pl.when(section < sections - 1)
-            def _():
-                hop(m, c).start()
+        mid = heads_width // 2
+        for first in (0, mid):
+            for g in range(first // GROUP, (first + mid) // GROUP):
+                each_side(lambda side: halo(m, g, side).wait_recv(), 0, 1)
+            for qcol in range(first, first + mid, HDIM):
+                kcol = qcol // GROUP * pair + qcol % GROUP
+                vcol = kcol + GROUP
+                scores = lax.dot_general(
+                    qbuf[m, :, qcol:qcol + HDIM], kv[m, :, kcol:kcol + HDIM], (((1,), (1,)), ((), ())),
+                    preferred_element_type=F32,
+                )
+                scores = jnp.where(allowed, scores, -1e30)
+                weights = jnp.exp2((scores - jnp.max(scores, axis=-1, keepdims=True)) * scale)
+                total_weight = jnp.sum(weights, axis=-1, keepdims=True)
+                head = jnp.dot(weights.astype(BF), kv[m, :, vcol:vcol + HDIM], preferred_element_type=F32)
+                mixed[:, qcol:qcol + HDIM] = (head / total_weight).astype(BF)
+            for c in range(chunks):
+                part, col = c * chunk // heads_width, c * chunk % heads_width
+                w = wall[3, first // half:(first + mid) // half, part * half:(part + 1) * half, col:col + chunk]
+                cols = slice(c * chunk, (c + 1) * chunk)
+                projection = jnp.dot(mixed[:, first:first + mid], w.reshape(mid, chunk), preferred_element_type=F32)
+                if first == 0:
+                    total[:, cols] = projection
+                    continue
+                projection = total[:, cols] + projection
+                hid[m, :, cols] = (xin[m, :, cols].astype(F32) + valid * projection).astype(BF)
+
+                @pl.when(section < sections - 1)
+                def _():
+                    hop(m, c).start()
 
         pltpu.make_async_copy(hid.at[m], out.at[0, m], out_sem.at[m]).start()
 
@@ -421,6 +425,7 @@
             pltpu.VMEM((rows, width), BF),
             pltpu.VMEM((micros, rows, heads_width), BF),
             pltpu.VMEM((rows, heads_width), BF),
+            pltpu.VMEM((rows, width), F32),
             pltpu.VMEM((micros, rows, width), BF),
             pltpu.VMEM(norm_gain.shape, BF),
             pltpu.SMEM((micros,), jnp.int32),

time: 213 us -> 212 us (level)
  no operation moved by 1% of the time
where the time goes in v4:
time: 212 us; the launch traced here: 211 us
  Pallas kernels  208 us (98%)
  local copies, waits for them, and re-layouts  3.16 us (1%)
    pallas_call x1, Pallas kernels, on_device(): pl.pallas_call(kernel, out_shape=jax.ShapeDtypeStruct((1, micros, rows, w...  208 us

profile of v4, /device:TPU:15, one launch (start us, length us, event | category | flops | bytes accessed | tf_op | source)
XLA Modules:
  0.0 211.4 jit_solution(8232583558546626876)
XLA Ops:
  0.0 208.3 %relay.1 = bf16[1,4,128,2048]{3,2,1,0:T(8,128)(2,1)} custom-call(bf16[4,128,2048]{2,1,0:T(8,128)(2,1)} %frames.1, bf16[1,2048]{1,0:T(2,128)(2,1)} %gain_hbm.1, bf16[1,64,3072]{2,1,0:T(8,128)(2,1)} %w_qkv.1, bf16[1,32,2048]{2,1,0:T(8,128)(2,1)} %w_out.1, s32[4]{0:T(128)} %bitcast.1, s32[8]{0:T(128)} %windows_hbm.1, s32[8]{0:T(128)} %shifts_hbm.1), custom_call_target="tpu_custom_call" | custom-call | tf_op jit(solution)/shard_map/relay/pallas_call | solution.py:415
  208.3 3.2 %copy.9 = bf16[1,4,128,2048]{3,2,1,0:T(8,128)(2,1)} copy(bf16[1,4,128,2048]{3,2,1,0:T(8,128)(2,1)} %relay.1) | data formatting | bytes 4194304
